TPU v7x, 256 devices: a whole 4x4x8 slice. The times are simulated.
256 devices in a mesh: dom: 64 (over z, y, core), rep: 4 (over x).
Axes of the slice: x: 4, y: 4, z: 8, core: 2. Of those that a mesh axis runs over, the one named last changes fastest.
Arguments:
- features: bfloat16 [65536, 512], P('dom', 'rep'), may hold values from -6 to 6
- weight: bfloat16 [512, 512], P(None, 'rep'), may hold values from -0.25 to 0.25
- bias: bfloat16 [512], P('rep'), may hold values from -3 to 3
- cotangent: bfloat16 [65536, 512], P('dom', 'rep'), may hold values from -6 to 6
- tile_vals: bfloat16 [64, 160, 128, 128], P('dom'), may hold values from -0.21875 to 0.21875
- tile_row: int32 [64, 160], P('dom'), may hold values from 0 to 8, as said below
- tile_src: int32 [64, 160], P('dom'), may hold values from 0 to 135, as said below
- send_blocks: int32 [64, 64, 2], P('dom'), may hold values from 0 to 7
- send_count: int32 [64, 64], P('dom'), may hold values from 0 to 2, as said below
Outputs:
- out: bfloat16 [65536, 512], P('dom', 'rep')
- grad_input: bfloat16 [65536, 512], P('dom', 'rep')
- grad_weight: float32 [512, 512], P(None, 'rep')
- grad_bias: float32 [512], P('rep')
Inputs may be any that keep to these rules, and one draw needn't show every extreme that they name: Partition q sends the first send_count[q, p] entries of send_blocks[q, p] to partition p; send_count[q, q] = 0, and every partition sends 2 blocks to some partition. `tile_row`: 8 marks an unused slot. Slots below 32 take own blocks; slot 32 + q * 2 + c is used only if c < send_count[q, p]. Partition 0 uses all its own-block slots. `tile_src`: slots below 32 name an own block below 8; slot 32 + m names source slot 8 + m.
All inputs are finite; a program needn't handle non-finite values.
Results may differ from a plain program's by a relative error of at most 0.007.
Values may be sent and summed in bfloat16 or wider, within the bound.
A program may use at most 128 MiB of HBM per device.

v0:
```python
import jax
import jax.numpy as jnp
from jax import lax
from jax.sharding import PartitionSpec as P

B = 128
NB = 8
CAP = 2


def receive_blocks(outgoing, peer_count, panel_width):
    arrived = lax.all_to_all(outgoing, "dom", split_axis=0, concat_axis=0, tiled=True)
    return arrived.reshape(peer_count * CAP, B, panel_width)


def shards(
    features, weight, bias, cotangent, tile_vals, tile_row, tile_src, send_blocks, send_count
):
    row_count, panel_width = features.shape
    peer_count = lax.axis_size("dom")
    gathered = lax.all_gather(features, "rep", axis=1, tiled=True)
    hidden = jnp.dot(gathered, weight, preferred_element_type=jnp.float32).astype(jnp.bfloat16)
    hidden_blocks = hidden.reshape(NB, B, panel_width)
    targets = send_blocks[0]
    counts = send_count[0]
    keep_slot = jnp.arange(CAP, dtype=jnp.int32)[None, :] < counts[:, None]
    outgoing = hidden_blocks[targets]
    outgoing = jnp.where(keep_slot[:, :, None, None], outgoing, jnp.zeros_like(outgoing))
    tile_set = tile_vals[0]
    tile_rows = tile_row[0]
    tile_sources = tile_src[0]
    arrived = receive_blocks(outgoing, peer_count, panel_width)
    sources = jnp.concatenate([hidden_blocks, arrived], 0)
    product = jnp.einsum(
        "kab,kbf->kaf", tile_set, sources[tile_sources], preferred_element_type=jnp.float32
    )
    aggregate = jax.ops.segment_sum(product, tile_rows, NB + 1)[:NB]
    shifted = aggregate.reshape(row_count, panel_width) + bias.astype(jnp.float32)
    sigma = jax.nn.sigmoid(shifted)
    out = (shifted * sigma).astype(jnp.bfloat16)
    grad_pre = (cotangent.astype(jnp.float32) * sigma * (1.0 + shifted * (1.0 - sigma))).astype(
        jnp.bfloat16
    )
    pre_padded = jnp.concatenate(
        [grad_pre.reshape(NB, B, panel_width), jnp.zeros((1, B, panel_width), jnp.bfloat16)], 0
    )
    contrib = jnp.einsum(
        "kab,kaf->kbf", tile_set, pre_padded[tile_rows], preferred_element_type=jnp.float32
    )
    per_slot = jax.ops.segment_sum(contrib, tile_sources, NB + peer_count * CAP)
    outbound = per_slot[NB:].reshape(peer_count, CAP, B, panel_width)
    returned = lax.all_to_all(outbound, "dom", split_axis=0, concat_axis=0, tiled=True)
    own_blocks = per_slot[:NB]
    returned = jnp.where(keep_slot[:, :, None, None], returned, jnp.zeros_like(returned))
    grad_blocks = own_blocks + jax.ops.segment_sum(
        returned.reshape(peer_count * CAP, B, panel_width), targets.reshape(-1), NB
    )
    grad_agg = grad_blocks.reshape(row_count, panel_width).astype(jnp.bfloat16)
    weight_part = jnp.dot(gathered.T, grad_agg, preferred_element_type=jnp.float32)
    bias_part = jnp.sum(grad_pre.astype(jnp.float32), 0)
    grad_weight, grad_bias = lax.psum((weight_part, bias_part), "dom")
    partial_terms = jnp.dot(grad_agg, weight.T, preferred_element_type=jnp.float32)
    grad_input = lax.psum_scatter(partial_terms, "rep", scatter_dimension=1, tiled=True).astype(
        jnp.bfloat16
    )
    return (out, grad_input, grad_weight, grad_bias)


def solution(mesh):
    in_specs = (
        P("dom", "rep"),
        P(None, "rep"),
        P("rep"),
        P("dom", "rep"),
        P("dom", None, None, None),
        P("dom", None),
        P("dom", None),
        P("dom", None, None),
        P("dom", None),
    )
    out_specs = (P("dom", "rep"), P("dom", "rep"), P(None, "rep"), P("rep"))
    return jax.shard_map(shards, mesh=mesh, in_specs=in_specs, out_specs=out_specs, check_vma=False)
```

profile of v0, /device:TPU:1, one launch (start us, length us, event | category | flops | bytes accessed | tf_op | source)
XLA Modules:
  0.0 723.8 jit_solution(12466726873163206390)
XLA Ops:
  7.9 0.7 compare_select_fusion.2
  8.9 0.7 iota_compare_fusion
  9.6 31.6 %all-gather.2.cloned.1.call-done = bf16[1024,512]{1,0:T(8,128)(2,1)} async-done(((bf16[1024,128]{1,0:T(8,128)(2,1)}), bf16[1024,512]{1,0:T(8,128)(2,1)}) %all-gather.2.cloned.1.call-update) | async-done | bytes 1048592 | tf_op jit(solution)/shard_map/all_gather | solution.py:21
  41.2 1.7 convolution_convert_fusion
  42.8 3.0 gather_fusion
  45.9 4.5 broadcast_select_fusion.1
  50.4 11.9 %all-to-all-start = ((bf16[64,2,128,128]{3,2,1,0:T(8,128)(2,1)}), bf16[64,2,128,128]{3,2,1,0:T(8,128)(2,1)}, u32[]{:S(2)}, u32[]{:S(2)}) async-start(bf16[64,2,128,128]{3,2,1,0:T(8,128)(2,1)} %broadcast_select_fusion.1), calls=%async_computation | async-start | bytes 8388608 | tf_op jit(solution)/shard_map/all_to_all | solution.py:12
  62.4 94.3 %all-to-all-done = bf16[64,2,128,128]{3,2,1,0:T(8,128)(2,1)} async-done(((bf16[64,2,128,128]{3,2,1,0:T(8,128)(2,1)}), bf16[64,2,128,128]{3,2,1,0:T(8,128)(2,1)}, u32[]{:S(2)}, u32[]{:S(2)}) %all-to-all-start) | async-done | bytes 4194336 | tf_op jit(solution)/shard_map/all_to_all | solution.py:12
  156.7 4.6 pad_maximum_fusion
  161.3 10.0 %gather_fusion.1 = bf16[160,128,128]{2,1,0:T(8,128)(2,1)} fusion(bf16[136,128,128]{2,1,0:T(8,128)(2,1)} %pad_maximum_fusion, s32[1024]{0:T(1024)S(1)} %pad_clamp_fusion.1), kind=kCustom, calls=%fused_computation.1 | custom fusion | bytes 10486400 | tf_op jit(solution)/shard_map/gather | solution.py:35
  171.3 11.8 %fusion.4 = f32[160,128,128]{1,2,0:T(8,128)} fusion(bf16[160,128,128]{2,1,0:T(8,128)(2,1)} %gather_fusion.1, bf16[1,160,128,128]{3,2,1,0:T(8,128)(2,1)} %param.13), kind=kOutput, calls=%fused_computation.13 | convolution fusion | flops 671088640 | bytes 20971520 | tf_op jit(solution)/shard_map/kab,kbf->kaf/dot_general | solution.py:34
  183.2 11.7 %copy.20 = f32[160,128,128]{2,1,0:T(8,128)} copy(f32[160,128,128]{1,2,0:T(8,128)} %fusion.4) | data formatting | bytes 20971520 | tf_op jit(solution)/shard_map/kab,kbf->kaf/dot_general | solution.py:34
  194.9 21.1 %scatter_fusion = f32[9,128,128]{2,1,0:T(8,128)S(1)} fusion(f32[9,128,128]{2,1,0:T(8,128)S(1)} %broadcast_in_dim.19, s32[160]{0:T(256)S(1)} %bitcast.58, f32[160,128,128]{2,1,0:T(8,128)} %copy.20), kind=kCustom, calls=%fused_computation.3 | custom fusion | flops 2621440 | bytes 31457920 | tf_op jit(solution)/shard_map/scatter-add | solution.py:37
  216.2 1.0 convert_reduce_fusion
  217.2 7.5 %gather_fusion.2 = bf16[160,128,128]{2,1,0:T(8,128)(2,1)} fusion(bf16[9,128,128]{2,1,0:T(8,128)(2,1)S(1)} %concatenate.7, s32[1024]{0:T(1024)S(1)} %pad_clamp_fusion), kind=kCustom, calls=%fused_computation.2 | custom fusion | bytes 10486400 | tf_op jit(solution)/shard_map/gather | solution.py:48
  224.6 9.8 %fusion.7 = f32[160,128,128]{1,2,0:T(8,128)} fusion(bf16[160,128,128]{2,1,0:T(8,128)(2,1)} %gather_fusion.2, bf16[1,160,128,128]{3,2,1,0:T(8,128)(2,1)} %param.13), kind=kOutput, calls=%fused_computation.14 | convolution fusion | flops 671088640 | bytes 20971520 | tf_op jit(solution)/shard_map/kab,kaf->kbf/dot_general | solution.py:47
  234.4 11.8 %copy.22 = f32[160,128,128]{2,1,0:T(8,128)} copy(f32[160,128,128]{1,2,0:T(8,128)} %fusion.7) | data formatting | bytes 20971520 | tf_op jit(solution)/shard_map/kab,kaf->kbf/dot_general | solution.py:47
  246.2 4.6 broadcast_in_dim.38
  250.8 33.2 %scatter_fusion.1 = f32[136,128,128]{2,1,0:T(8,128)} fusion(f32[136,128,128]{2,1,0:T(8,128)} %broadcast_in_dim.38, s32[160]{0:T(256)S(1)} %bitcast.59, f32[160,128,128]{2,1,0:T(8,128)} %copy.22), kind=kCustom, calls=%fused_computation.4 | custom fusion | flops 2621440 | bytes 31457920 | tf_op jit(solution)/shard_map/scatter-add | solution.py:50
  284.0 7.9 %slice.20 = f32[128,128,128]{2,1,0:T(8,128)} slice(f32[136,128,128]{2,1,0:T(8,128)} %scatter_fusion.1), slice={[8:136], [0:128], [0:128]} | slice | bytes 16777216 | tf_op jit(solution)/shard_map/slice | solution.py:51
  291.8 7.6 %all-to-all-start.1 = ((f32[64,2,128,128]{3,2,1,0:T(8,128)}), f32[64,2,128,128]{3,2,1,0:T(8,128)}, u32[]{:S(2)}, u32[]{:S(2)}) async-start(f32[64,2,128,128]{3,2,1,0:T(8,128)} %bitcast.52), calls=%async_computation.1 | async-start | bytes 16777216 | tf_op jit(solution)/shard_map/all_to_all | solution.py:52
  299.7 1.1 slice.19
  300.8 181.5 %all-to-all-done.1 = f32[64,2,128,128]{3,2,1,0:T(8,128)} async-done(((f32[64,2,128,128]{3,2,1,0:T(8,128)}), f32[64,2,128,128]{3,2,1,0:T(8,128)}, u32[]{:S(2)}, u32[]{:S(2)}) %all-to-all-start.1) | async-done | bytes 8388640 | tf_op jit(solution)/shard_map/all_to_all | solution.py:52
  482.3 7.2 broadcast_select_fusion
  489.6 17.0 %scatter_fusion.2 = f32[8,128,128]{2,1,0:T(8,128)S(1)} fusion(f32[8,128,128]{2,1,0:T(8,128)S(1)} %slice.19, s32[128]{0:T(128)S(1)} %reshape.185, f32[128,128,128]{2,1,0:T(8,128)} %bitcast.53), kind=kCustom, calls=%fused_computation.5 | custom fusion | flops 2097152 | bytes 25166336 | tf_op jit(solution)/shard_map/scatter-add | solution.py:55
  506.6 1.0 convolution_bitcast_fusion
  507.7 1.8 fusion.10
  509.6 127.7 %psum.15 = f32[128]{0:T(128)} all-reduce(f32[128]{0:T(128)S(1)} %get-tuple-element.12), channel_id=1, replica_groups=mesh['dom'=64,'rep'=4] {'dom'}, use_global_device_ids=true, to_apply=%region_6.7 | all-reduce | flops 128 | bytes 1024 | tf_op jit(solution)/shard_map/psum | solution.py:61
  637.3 46.1 %all-reduce.3.cloned.1.call-done = f32[512,128]{0,1:T(8,128)} async-done(((f32[512,128]{0,1:T(8,128)}), f32[512,128]{0,1:T(8,128)}) %all-reduce.3.cloned.1.call-update) | async-done | bytes 262160 | tf_op jit(solution)/shard_map/psum | solution.py:61
  683.4 1.8 copy.24
  685.1 30.4 %reduce-scatter.2.cloned.1.call-done = f32[1024,128]{1,0:T(8,128)} async-done(((f32[1024,512]{1,0:T(8,128)}), f32[1024,128]{1,0:T(8,128)}) %reduce-scatter.2.cloned.1.call-update) | async-done | bytes 524304 | tf_op jit(solution)/shard_map/reduce_scatter | solution.py:63
  715.5 1.8 convert_element_type.34
  (34 shorter events, 1.5 us)
Async XLA Ops:
  7.2 34.0 %copy-start = (bf16[512,128]{1,0:T(8,128)(2,1)S(1)}, bf16[512,128]{1,0:T(8,128)(2,1)}, u32[]{:S(2)}) copy-start(bf16[512,128]{1,0:T(8,128)(2,1)} %param.10) | copy-start | bytes 393220
  7.2 34.0 %all-gather.2.cloned.1.call-start = ((), (), s32[]{:S(2)}) async-start(), calls=%async_computation.3 | async-start | bytes 1310720 | tf_op jit(solution)/shard_map/all_gather | solution.py:21
  50.4 11.9 %copy-start.6 = (bf16[128]{0:T(256)(128)(2,1)S(1)}, bf16[128]{0:T(256)(128)(2,1)}, u32[]{:S(2)}) copy-start(bf16[128]{0:T(256)(128)(2,1)} %param.11) | copy-start | bytes 772
  50.4 11.9 %copy-start.4 = (s32[1,160]{1,0:T(1,128)S(1)}, s32[1,160]{1,0:T(1,128)}, u32[]{:S(2)}) copy-start(s32[1,160]{1,0:T(1,128)} %param.15) | copy-start | bytes 1924
  50.4 12.0 %copy-start.3 = (s32[1,160]{1,0:T(1,128)S(1)}, s32[1,160]{1,0:T(1,128)}, u32[]{:S(2)}) copy-start(s32[1,160]{1,0:T(1,128)} %param.14) | copy-start | bytes 1924
  50.4 106.3 %all-to-all-start = ((bf16[64,2,128,128]{3,2,1,0:T(8,128)(2,1)}), bf16[64,2,128,128]{3,2,1,0:T(8,128)(2,1)}, u32[]{:S(2)}, u32[]{:S(2)}) async-start(bf16[64,2,128,128]{3,2,1,0:T(8,128)(2,1)} %broadcast_select_fusion.1), calls=%async_computation | async-start | bytes 8388608 | tf_op jit(solution)/shard_map/all_to_all | solution.py:12
  194.9 21.2 %copy-start.2 = (bf16[1024,128]{1,0:T(8,128)(2,1)S(1)}, bf16[1024,128]{1,0:T(8,128)(2,1)}, u32[]{:S(2)}) copy-start(bf16[1024,128]{1,0:T(8,128)(2,1)} %param.12) | copy-start | bytes 786436
  291.8 7.7 %copy-start.5 = (s32[1,64,2]{1,2,0:T(2,128)S(1)}, s32[1,64,2]{1,2,0:T(2,128)}, u32[]{:S(2)}) copy-start(s32[1,64,2]{1,2,0:T(2,128)} %param.16) | copy-start | bytes 1540
  291.8 190.5 %all-to-all-start.1 = ((f32[64,2,128,128]{3,2,1,0:T(8,128)}), f32[64,2,128,128]{3,2,1,0:T(8,128)}, u32[]{:S(2)}, u32[]{:S(2)}) async-start(f32[64,2,128,128]{3,2,1,0:T(8,128)} %bitcast.52), calls=%async_computation.1 | async-start | bytes 16777216 | tf_op jit(solution)/shard_map/all_to_all | solution.py:52
  299.4 383.9 %all-reduce.3.cloned.1.call-start = ((), (), s32[]{:S(2)}) async-start(), calls=%async_computation.5 | async-start | bytes 524288 | tf_op jit(solution)/shard_map/psum | solution.py:61
  489.5 17.1 %copy-start.1 = (bf16[1024,512]{1,0:T(8,128)(2,1)S(1)}, bf16[1024,512]{1,0:T(8,128)(2,1)}, u32[]{:S(2)}) copy-start(bf16[1024,512]{1,0:T(8,128)(2,1)} %all-gather.2.cloned.1.call-done) | copy-start | bytes 3145732
  507.7 207.8 %reduce-scatter.2.cloned.1.call-start = ((), (), s32[]{:S(2)}) async-start(), calls=%async_computation.4 | async-start | bytes 2621440 | tf_op jit(solution)/shard_map/reduce_scatter | solution.py:63
Sparse Core Ops, SparseCore 0:
  9.8 31.3 all-gather.1
  507.8 175.4 all-reduce.2
  686.1 29.4 reduce-scatter.1
where the time goes:
time: 726 us; the launch traced here: 724 us
  waiting for transfers between devices  385 us (53%)
  blocking collectives  128 us (18%)
  other arithmetic  91.9 us (13%)
  local copies, waits for them, and re-layouts  60 us (8%)
  matrix products  26.1 us (4%)
  starting transfers between devices  19.6 us (3%)
  between operations  13.9 us (2%)
    all_to_all x1, waiting for transfers between devices, shards(): lax.all_to_all(outbound, 'dom', split_axis=0, concat_axis=0, tiled=True)  182 us
    psum x1, blocking collectives, shards(): grad_weight, grad_bias = lax.psum((weight_part, bias_part), 'dom')  128 us
    all_to_all x1, waiting for transfers between devices, receive_blocks(): lax.all_to_all(outgoing, 'dom', split_axis=0, concat_axis=0, tiled=True)  94.3 us
    psum x1, waiting for transfers between devices, shards(): grad_weight, grad_bias = lax.psum((weight_part, bias_part), 'dom')  46.1 us
    scatter-add x1, other arithmetic, shards(): per_slot = jax.ops.segment_sum(contrib, tile_sources, NB + peer_count * CAP)  33.2 us
    all_gather x1, waiting for transfers between devices, shards(): gathered = lax.all_gather(features, 'rep', axis=1, tiled=True)  31.6 us
    reduce_scatter x1, waiting for transfers between devices, shards(): lax.psum_scatter(partial_terms, 'rep', scatter_dimension=1, tiled=True)  30.4 us
    scatter-add x1, other arithmetic, shards(): aggregate = jax.ops.segment_sum(product, tile_rows, NB + 1)[:NB]  21.1 us
  transfers between devices with their start and end apart: 5, of which 5 were waited for; matrix products, arithmetic and copies ran while one was open for 1% of the time, Pallas kernels for 0%

commit v1 on v0

--- a/solution.py
+++ b/solution.py
@@ -1,3 +1,4 @@
+import functools
 import jax
 import jax.numpy as jnp
 from jax import lax
@@ -6,6 +7,19 @@
 B = 128
 NB = 8
 CAP = 2
+
+
+def roads_render(x0, lane_axis):
+    formed = jnp.concatenate(
+        lax.all_to_all(
+            jnp.stack(lax.axis_size(lane_axis) * [x0]), lane_axis, split_axis=0, concat_axis=0
+        ),
+        1,
+    )
+    return formed
+
+
+open_the_sheet = functools.partial(roads_render, lane_axis="rep")
 
 
 def receive_blocks(outgoing, peer_count, panel_width):
@@ -18,7 +32,7 @@
 ):
     row_count, panel_width = features.shape
     peer_count = lax.axis_size("dom")
-    gathered = lax.all_gather(features, "rep", axis=1, tiled=True)
+    gathered = open_the_sheet(features)
     hidden = jnp.dot(gathered, weight, preferred_element_type=jnp.float32).astype(jnp.bfloat16)
     hidden_blocks = hidden.reshape(NB, B, panel_width)
     targets = send_blocks[0]

time: 726 us -> 684 us (0.942)
  waiting for transfers between devices: 385 us -> 332 us
  starting transfers between devices: 19.6 us -> 27.4 us
    all_gather x1 -> x0, waiting for transfers between devices: 31.6 us -> none  [shards(): gathered = lax.all_gather(features, 'rep', axis=1, tiled=True)]
    reduce_scatter x1, waiting for transfers between devices: 30.4 us -> 0.01 us  [shards(): lax.psum_scatter(partial_terms, 'rep', scatter_dimension=1, tiled=True)]
    all_to_all x0 -> x1, waiting for transfers between devices: none -> 11.6 us  [roads_render(): lax.all_to_all(jnp.stack(lax.axis_size(lane_axis) * [x0]), lane_axis, spl...]
  transfers between devices with their start and end apart: 5 -> 5, of which waited for: 5 -> 4; matrix products, arithmetic and copies ran while one was open for 1% -> 1% of each run, Pallas kernels for 0% -> 0%
where the time goes in v1:
time: 684 us; the launch traced here: 682 us
  waiting for transfers between devices  332 us (49%)
  blocking collectives  128 us (19%)
  other arithmetic  91.7 us (13%)
  local copies, waits for them, and re-layouts  62.2 us (9%)
  starting transfers between devices  27.4 us (4%)
  matrix products  25.1 us (4%)
  between operations  15.7 us (2%)
    all_to_all x1, waiting for transfers between devices, shards(): lax.all_to_all(outbound, 'dom', split_axis=0, concat_axis=0, tiled=True)  182 us
    psum x1, blocking collectives, shards(): grad_weight, grad_bias = lax.psum((weight_part, bias_part), 'dom')  128 us
    all_to_all x1, waiting for transfers between devices, receive_blocks(): lax.all_to_all(outgoing, 'dom', split_axis=0, concat_axis=0, tiled=True)  94.3 us
    psum x1, waiting for transfers between devices, shards(): grad_weight, grad_bias = lax.psum((weight_part, bias_part), 'dom')  44.9 us
    scatter-add x1, other arithmetic, shards(): per_slot = jax.ops.segment_sum(contrib, tile_sources, NB + peer_count * CAP)  33.1 us
    scatter-add x1, other arithmetic, shards(): aggregate = jax.ops.segment_sum(product, tile_rows, NB + 1)[:NB]  21.1 us
    scatter-add x1, other arithmetic, shards(): jax.ops.segment_sum(returned.reshape(peer_count * CAP, B, panel_width), t...  17 us
    all_to_all x1, starting transfers between devices, receive_blocks(): lax.all_to_all(outgoing, 'dom', split_axis=0, concat_axis=0, tiled=True)  14.8 us
  transfers between devices with their start and end apart: 5, of which 4 were waited for; matrix products, arithmetic and copies ran while one was open for 1% of the time, Pallas kernels for 0%

profile of v1, /device:TPU:1, one launch (start us, length us, event | category | flops | bytes accessed | tf_op | source)
XLA Modules:
  0.0 682.2 jit_solution(9730330559220744480)
XLA Ops:
  8.0 1.1 copy.18
  9.1 1.1 stack.2
  10.3 4.8 all-to-all-start
  16.0 0.7 iota_compare_fusion
  16.8 11.6 %all-to-all-done = bf16[4,1024,128]{1,2,0:T(8,128)(2,1)S(1)} async-done(((bf16[4,1024,128]{1,2,0:T(8,128)(2,1)}), bf16[4,1024,128]{1,2,0:T(8,128)(2,1)S(1)}, u32[]{:S(2)}, u32[]{:S(2)}) %all-to-all-start) | async-done | bytes 1048608 | tf_op jit(solution)/shard_map/all_to_all | solution.py:14
  28.8 3.1 gather_fusion
  31.9 4.5 broadcast_select_fusion.1
  36.4 14.8 %all-to-all-start.1 = ((bf16[64,2,128,128]{3,2,1,0:T(8,128)(2,1)}), bf16[64,2,128,128]{3,2,1,0:T(8,128)(2,1)}, u32[]{:S(2)}, u32[]{:S(2)}) async-start(bf16[64,2,128,128]{3,2,1,0:T(8,128)(2,1)} %broadcast_select_fusion.1), calls=%async_computation.1 | async-start | bytes 8388608 | tf_op jit(solution)/shard_map/all_to_all | solution.py:26
  51.3 94.3 %all-to-all-done.1 = bf16[64,2,128,128]{3,2,1,0:T(8,128)(2,1)} async-done(((bf16[64,2,128,128]{3,2,1,0:T(8,128)(2,1)}), bf16[64,2,128,128]{3,2,1,0:T(8,128)(2,1)}, u32[]{:S(2)}, u32[]{:S(2)}) %all-to-all-start.1) | async-done | bytes 4194336 | tf_op jit(solution)/shard_map/all_to_all | solution.py:26
  145.6 4.6 pad_maximum_fusion
  150.2 10.0 %gather_fusion.1 = bf16[160,128,128]{2,1,0:T(8,128)(2,1)} fusion(bf16[136,128,128]{2,1,0:T(8,128)(2,1)} %pad_maximum_fusion, s32[1024]{0:T(1024)S(1)} %pad_clamp_fusion.1), kind=kCustom, calls=%fused_computation.1 | custom fusion | bytes 10486400 | tf_op jit(solution)/shard_map/gather | solution.py:49
  160.2 11.8 %fusion.4 = f32[160,128,128]{1,2,0:T(8,128)} fusion(bf16[160,128,128]{2,1,0:T(8,128)(2,1)} %gather_fusion.1, bf16[1,160,128,128]{3,2,1,0:T(8,128)(2,1)} %param.13), kind=kOutput, calls=%fused_computation.13 | convolution fusion | flops 671088640 | bytes 20971520 | tf_op jit(solution)/shard_map/kab,kbf->kaf/dot_general | solution.py:48
  172.0 11.7 %copy.21 = f32[160,128,128]{2,1,0:T(8,128)} copy(f32[160,128,128]{1,2,0:T(8,128)} %fusion.4) | data formatting | bytes 20971520 | tf_op jit(solution)/shard_map/kab,kbf->kaf/dot_general | solution.py:48
  183.8 21.1 %scatter_fusion = f32[9,128,128]{2,1,0:T(8,128)S(1)} fusion(f32[9,128,128]{2,1,0:T(8,128)S(1)} %broadcast_in_dim.19, s32[160]{0:T(256)S(1)} %bitcast.63, f32[160,128,128]{2,1,0:T(8,128)} %copy.21), kind=kCustom, calls=%fused_computation.3 | custom fusion | flops 2621440 | bytes 31457920 | tf_op jit(solution)/shard_map/scatter-add | solution.py:51
  205.0 1.0 convert_reduce_fusion
  206.0 7.5 %gather_fusion.2 = bf16[160,128,128]{2,1,0:T(8,128)(2,1)} fusion(bf16[9,128,128]{2,1,0:T(8,128)(2,1)S(1)} %concatenate.7, s32[1024]{0:T(1024)S(1)} %pad_clamp_fusion), kind=kCustom, calls=%fused_computation.2 | custom fusion | bytes 10486400 | tf_op jit(solution)/shard_map/gather | solution.py:62
  213.5 9.8 %fusion.7 = f32[160,128,128]{1,2,0:T(8,128)} fusion(bf16[160,128,128]{2,1,0:T(8,128)(2,1)} %gather_fusion.2, bf16[1,160,128,128]{3,2,1,0:T(8,128)(2,1)} %param.13), kind=kOutput, calls=%fused_computation.14 | convolution fusion | flops 671088640 | bytes 20971520 | tf_op jit(solution)/shard_map/kab,kaf->kbf/dot_general | solution.py:61
  223.3 11.8 %copy.23 = f32[160,128,128]{2,1,0:T(8,128)} copy(f32[160,128,128]{1,2,0:T(8,128)} %fusion.7) | data formatting | bytes 20971520 | tf_op jit(solution)/shard_map/kab,kaf->kbf/dot_general | solution.py:61
  235.1 4.6 broadcast_in_dim.38
  239.7 33.1 %scatter_fusion.1 = f32[136,128,128]{2,1,0:T(8,128)} fusion(f32[136,128,128]{2,1,0:T(8,128)} %broadcast_in_dim.38, s32[160]{0:T(256)S(1)} %bitcast.64, f32[160,128,128]{2,1,0:T(8,128)} %copy.23), kind=kCustom, calls=%fused_computation.4 | custom fusion | flops 2621440 | bytes 31457920 | tf_op jit(solution)/shard_map/scatter-add | solution.py:64
  272.7 7.9 %slice.20 = f32[128,128,128]{2,1,0:T(8,128)} slice(f32[136,128,128]{2,1,0:T(8,128)} %scatter_fusion.1), slice={[8:136], [0:128], [0:128]} | slice | bytes 16777216 | tf_op jit(solution)/shard_map/slice | solution.py:65
  280.6 7.7 %all-to-all-start.2 = ((f32[64,2,128,128]{3,2,1,0:T(8,128)}), f32[64,2,128,128]{3,2,1,0:T(8,128)}, u32[]{:S(2)}, u32[]{:S(2)}) async-start(f32[64,2,128,128]{3,2,1,0:T(8,128)} %bitcast.55), calls=%async_computation.2 | async-start | bytes 16777216 | tf_op jit(solution)/shard_map/all_to_all | solution.py:66
  288.6 1.1 slice.19
  289.7 181.5 %all-to-all-done.2 = f32[64,2,128,128]{3,2,1,0:T(8,128)} async-done(((f32[64,2,128,128]{3,2,1,0:T(8,128)}), f32[64,2,128,128]{3,2,1,0:T(8,128)}, u32[]{:S(2)}, u32[]{:S(2)}) %all-to-all-start.2) | async-done | bytes 8388640 | tf_op jit(solution)/shard_map/all_to_all | solution.py:66
  471.2 7.2 %broadcast_select_fusion = f32[64,2,128,128]{3,2,1,0:T(8,128)} fusion(f32[64,2,128,128]{3,2,1,0:T(8,128)} %all-to-all-done.2, pred[64,2]{1,0:T(8,128)(4,1)S(1)} %iota_compare_fusion), kind=kLoop, calls=%fused_computation.11 | loop fusion | flops 2097152 | bytes 16777344 | tf_op jit(solution)/shard_map/jit(_where)/select_n | solution.py:68
  478.4 17.0 %scatter_fusion.2 = f32[8,128,128]{2,1,0:T(8,128)S(1)} fusion(f32[8,128,128]{2,1,0:T(8,128)S(1)} %slice.19, s32[128]{0:T(128)S(1)} %reshape.196, f32[128,128,128]{2,1,0:T(8,128)} %bitcast.56), kind=kCustom, calls=%fused_computation.5 | custom fusion | flops 2097152 | bytes 25166336 | tf_op jit(solution)/shard_map/scatter-add | solution.py:69
  495.5 1.2 convolution_bitcast_fusion
  496.7 1.8 fusion.10
  498.5 127.7 %psum.15 = f32[128]{0:T(128)} all-reduce(f32[128]{0:T(128)S(1)} %get-tuple-element.12), channel_id=1, replica_groups=mesh['dom'=64,'rep'=4] {'dom'}, use_global_device_ids=true, to_apply=%region_6.7 | all-reduce | flops 128 | bytes 1024 | tf_op jit(solution)/shard_map/psum | solution.py:75
  626.3 44.9 %all-reduce.3.cloned.1.call-done = f32[512,128]{0,1:T(8,128)} async-done(((f32[512,128]{0,1:T(8,128)}), f32[512,128]{0,1:T(8,128)}) %all-reduce.3.cloned.1.call-update) | async-done | bytes 262160 | tf_op jit(solution)/shard_map/psum | solution.py:75
  671.2 1.8 copy.25
  673.0 1.8 convert_element_type.35
  (33 shorter events, 2.0 us)
Async XLA Ops:
  8.0 20.3 %copy-start = (bf16[512,128]{1,0:T(8,128)(2,1)S(1)}, bf16[512,128]{1,0:T(8,128)(2,1)}, u32[]{:S(2)}) copy-start(bf16[512,128]{1,0:T(8,128)(2,1)} %param.10) | copy-start | bytes 393220
  10.3 18.1 %all-to-all-start = ((bf16[4,1024,128]{1,2,0:T(8,128)(2,1)}), bf16[4,1024,128]{1,2,0:T(8,128)(2,1)S(1)}, u32[]{:S(2)}, u32[]{:S(2)}) async-start(bf16[4,1024,128]{1,2,0:T(8,128)(2,1)} %stack.2), calls=%async_computation | async-start | bytes 2097152 | tf_op jit(solution)/shard_map/all_to_all | solution.py:14
  36.4 14.8 %copy-start.5 = (bf16[128]{0:T(256)(128)(2,1)S(1)}, bf16[128]{0:T(256)(128)(2,1)}, u32[]{:S(2)}) copy-start(bf16[128]{0:T(256)(128)(2,1)} %param.11) | copy-start | bytes 772
  36.4 14.8 %copy-start.3 = (s32[1,160]{1,0:T(1,128)S(1)}, s32[1,160]{1,0:T(1,128)}, u32[]{:S(2)}) copy-start(s32[1,160]{1,0:T(1,128)} %param.15) | copy-start | bytes 1924
  36.4 14.9 %copy-start.2 = (s32[1,160]{1,0:T(1,128)S(1)}, s32[1,160]{1,0:T(1,128)}, u32[]{:S(2)}) copy-start(s32[1,160]{1,0:T(1,128)} %param.14) | copy-start | bytes 1924
  36.4 109.2 %all-to-all-start.1 = ((bf16[64,2,128,128]{3,2,1,0:T(8,128)(2,1)}), bf16[64,2,128,128]{3,2,1,0:T(8,128)(2,1)}, u32[]{:S(2)}, u32[]{:S(2)}) async-start(bf16[64,2,128,128]{3,2,1,0:T(8,128)(2,1)} %broadcast_select_fusion.1), calls=%async_computation.1 | async-start | bytes 8388608 | tf_op jit(solution)/shard_map/all_to_all | solution.py:26
  183.8 21.2 %copy-start.1 = (bf16[1024,128]{1,0:T(8,128)(2,1)S(1)}, bf16[1024,128]{1,0:T(8,128)(2,1)}, u32[]{:S(2)}) copy-start(bf16[1024,128]{1,0:T(8,128)(2,1)} %param.12) | copy-start | bytes 786436
  280.6 7.7 %copy-start.4 = (s32[1,64,2]{1,2,0:T(2,128)S(1)}, s32[1,64,2]{1,2,0:T(2,128)}, u32[]{:S(2)}) copy-start(s32[1,64,2]{1,2,0:T(2,128)} %param.16) | copy-start | bytes 1540
  280.6 190.6 %all-to-all-start.2 = ((f32[64,2,128,128]{3,2,1,0:T(8,128)}), f32[64,2,128,128]{3,2,1,0:T(8,128)}, u32[]{:S(2)}, u32[]{:S(2)}) async-start(f32[64,2,128,128]{3,2,1,0:T(8,128)} %bitcast.55), calls=%async_computation.2 | async-start | bytes 16777216 | tf_op jit(solution)/shard_map/all_to_all | solution.py:66
  288.3 382.9 %all-reduce.3.cloned.1.call-start = ((), (), s32[]{:S(2)}) async-start(), calls=%async_computation.5 | async-start | bytes 524288 | tf_op jit(solution)/shard_map/psum | solution.py:75
  496.7 176.3 %reduce-scatter.2.cloned.1.call-start = ((), (), s32[]{:S(2)}) async-start(), calls=%async_computation.4 | async-start | bytes 2621440 | tf_op jit(solution)/shard_map/reduce_scatter | solution.py:77
Sparse Core Ops, SparseCore 0:
  496.8 174.3 all-reduce.2
Sparse Core Ops, SparseCore 1:
  499.7 30.5 reduce-scatter.1
